TPU v7x, 32 devices: a whole 2x2x4 slice. The times are simulated.
32 devices in a mesh: parts: 2 (over y), blk: 2 (over core), group: 8 (over z, x).
Axes of the slice: x: 2, y: 2, z: 4, core: 2. Of those that a mesh axis runs over, the one named last changes fastest.
Arguments:
- img_student: bfloat16 [2048, 256], P(('parts', 'group')), parts along dimension 0, may hold values from -25 to 25
- txt_student: bfloat16 [2048, 256], P(('parts', 'group')), parts along dimension 0, may hold values from -25 to 25
- img_teacher: bfloat16 [2048, 512], P(('parts', 'group')), parts along dimension 0, may hold values from -25 to 25
- txt_teacher: bfloat16 [2048, 512], P(('parts', 'group')), parts along dimension 0, may hold values from -25 to 25
Outputs:
- grad_image: float32 [2048, 256], P(('parts', 'group')), parts along dimension 0
There are 2 independent parts, one for each index of `parts`. A program takes and returns all parts, laid end to end along the dimension named above; each array names one. Nothing has to cross between parts.
All inputs are finite; a program needn't handle non-finite values.
Results may differ from a plain program's by a relative error of at most 0.0028.
Values may be sent and summed in bfloat16 or wider, within the bound.
A program may use at most 128 MiB of HBM per device.

v0:
```python
import jax
import jax.numpy as jnp
from jax import lax
from jax.sharding import PartitionSpec as P


def merged_2(value, axis, join):
    pieces = jax.tree.map(lambda part: lax.all_gather(part, axis), value)
    head = jax.tree.map(lambda part: part[0], pieces)
    tail = jax.tree.map(lambda part: part[1:], pieces)
    so_far, _ = lax.scan(lambda so_far, piece: (join(so_far, piece), None), head, tail)
    return so_far


def combine(earlier, later):
    merged = []
    for which in (0, 2):
        highest = jnp.maximum(earlier[which], later[which])
        total = earlier[which + 1] * jnp.exp(earlier[which] - highest) + later[which + 1] * jnp.exp(
            later[which] - highest
        )
        merged.append(highest)
        merged.append(total)
    return tuple(merged)


def per_device(img_student, txt_student, img_teacher, txt_teacher):
    half_rows = img_student.shape[0] // 2
    side = lax.axis_index("blk")
    begin = side * half_rows
    text_student_own = lax.dynamic_slice_in_dim(txt_student, begin, half_rows, 0)
    text_teacher_own = lax.dynamic_slice_in_dim(txt_teacher, begin, half_rows, 0)
    contract = (((1,), (1,)), ((), ()))
    text_student, text_teacher = (
        lax.all_gather(text_student_own, "group", axis=0, tiled=True),
        lax.all_gather(text_teacher_own, "group", axis=0, tiled=True),
    )
    student = lax.dot_general(
        img_student, text_student, contract, preferred_element_type=jnp.float32
    )
    teacher = lax.dot_general(
        img_teacher, text_teacher, contract, preferred_element_type=jnp.float32
    )
    row_student_high = jnp.max(student, axis=1)
    row_teacher_high = jnp.max(teacher, axis=1)
    row_stats = (
        row_student_high,
        jnp.sum(jnp.exp(student - row_student_high[:, None]), axis=1),
        row_teacher_high,
        jnp.sum(jnp.exp(teacher - row_teacher_high[:, None]), axis=1),
    )
    row_all = merged_2(row_stats, "blk", combine)
    row_student = (row_all[0] + jnp.log(row_all[1]))[:, None]
    row_teacher = (row_all[2] + jnp.log(row_all[3]))[:, None]
    column_student_high = jnp.max(student, axis=0)
    column_teacher_high = jnp.max(teacher, axis=0)
    column_stats = (
        column_student_high,
        jnp.sum(jnp.exp(student - column_student_high[None, :]), axis=0),
        column_teacher_high,
        jnp.sum(jnp.exp(teacher - column_teacher_high[None, :]), axis=0),
    )
    totals = merged_2(column_stats, "group", combine)
    column_student = (totals[0] + jnp.log(totals[1]))[None, :]
    column_teacher = (totals[2] + jnp.log(totals[3]))[None, :]
    row_part = jnp.exp(student - row_student) - jnp.exp(teacher - row_teacher)
    column_part = jnp.exp(student - column_student) - jnp.exp(teacher - column_teacher)
    weights = (0.5 * (row_part + column_part)).astype(jnp.bfloat16)
    partial_image = jnp.dot(weights, text_student, preferred_element_type=jnp.float32)
    return lax.psum(partial_image, "blk")


def solution(mesh):
    placed = (
        P(("parts", "group"), None),
        P(("parts", "group"), None),
        P(("parts", "group"), None),
        P(("parts", "group"), None),
    )
    return jax.shard_map(
        per_device,
        mesh=mesh,
        in_specs=placed,
        out_specs=P(("parts", "group"), None),
        check_vma=False,
    )
```

profile of v0, /device:TPU:0, one launch (start us, length us, event | category | flops | bytes accessed | tf_op | source)
XLA Modules:
  0.0 214.9 jit_solution(7815627347188228653)
XLA Ops:
  6.5 0.8 constant_dynamic-slice_fusion.5
  7.3 32.6 %all_gather.54 = bf16[512,256]{1,0:T(8,128)(2,1)S(1)} all-gather(bf16[64,256]{1,0:T(8,128)(2,1)S(1)} %constant_dynamic-slice_fusion.5), channel_id=1, replica_groups=mesh['parts'=2,'blk'=2,'group'=8] {'group'}, dimensions={0}, use_global_device_ids=true | all-gather | bytes 294912 | tf_op jit(solution)/shard_map/all_gather | solution.py:35
  40.3 26.0 %all-gather.12 = f32[8,1,512]{2,1,0:T(1,128)S(1)} all-gather(f32[1,1,512]{2,1,0:T(1,128)S(1)} %bitcast.102), channel_id=6, replica_groups=mesh['parts'=2,'blk'=2,'group'=8] {'group'}, dimensions={0}, use_global_device_ids=true | all-gather | bytes 18432 | tf_op jit(solution)/shard_map/all_gather | solution.py:8
  66.3 0.6 copy-done.1
  67.2 26.0 %all-gather.13 = f32[8,1,512]{2,1,0:T(1,128)S(1)} all-gather(f32[1,1,512]{2,1,0:T(1,128)S(1)} %bitcast.103), channel_id=7, replica_groups=mesh['parts'=2,'blk'=2,'group'=8] {'group'}, dimensions={0}, use_global_device_ids=true | all-gather | bytes 18432 | tf_op jit(solution)/shard_map/all_gather | solution.py:8
  93.2 0.6 copy-done.2
  93.8 31.3 %all_gather.59 = bf16[512,512]{1,0:T(8,128)(2,1)S(1)} all-gather(bf16[64,512]{1,0:T(8,128)(2,1)S(1)} %constant_dynamic-slice_fusion.4), channel_id=1, replica_groups=mesh['parts'=2,'blk'=2,'group'=8] {'group'}, dimensions={0}, use_global_device_ids=true | all-gather | bytes 589824 | tf_op jit(solution)/shard_map/all_gather | solution.py:36
  125.1 0.4 fusion.11
  125.5 26.0 %all-gather.14 = f32[8,1,512]{2,1,0:T(1,128)S(1)} all-gather(f32[1,1,512]{2,1,0:T(1,128)S(1)} %bitcast.101), channel_id=8, replica_groups=mesh['parts'=2,'blk'=2,'group'=8] {'group'}, dimensions={0}, use_global_device_ids=true | all-gather | bytes 18432 | tf_op jit(solution)/shard_map/all_gather | solution.py:8
  151.5 0.6 copy-done.3
  152.4 26.0 %all-gather.15 = f32[8,1,512]{2,1,0:T(1,128)S(1)} all-gather(f32[1,1,512]{2,1,0:T(1,128)S(1)} %bitcast.104), channel_id=9, replica_groups=mesh['parts'=2,'blk'=2,'group'=8] {'group'}, dimensions={0}, use_global_device_ids=true | all-gather | bytes 18432 | tf_op jit(solution)/shard_map/all_gather | solution.py:8
  178.4 0.6 copy-done.4
  179.1 0.7 slice-done.3
  179.8 0.7 slice-done.5
  180.5 0.7 slice-done.7
  181.2 0.7 slice-done.2
  181.9 0.7 while.2
  182.7 1.8 all-gather.11
  184.4 1.8 all-gather.10
  186.2 1.8 all-gather.9
  187.9 1.8 all-gather.8
  189.8 1.1 fusion
  190.8 15.7 %all-reduce.2.cloned.1.call-done = f32[128,256]{1,0:T(8,128)} async-done(((f32[128,256]{1,0:T(8,128)}), f32[128,256]{1,0:T(8,128)}) %all-reduce.2.cloned.1.call-update) | async-done | bytes 131088 | tf_op jit(solution)/shard_map/psum | solution.py:70
  206.5 1.6 copy.35
  (70 shorter events, 1.5 us)
Async XLA Ops:
  6.5 118.6 %copy-start = (bf16[128,512]{1,0:T(8,128)(2,1)S(1)}, bf16[128,512]{1,0:T(8,128)(2,1)}, u32[]{:S(2)}) copy-start(bf16[128,512]{1,0:T(8,128)(2,1)} %param.8) | copy-start | bytes 393220
  6.5 200.0 %all-reduce.2.cloned.1.call-start = ((), (), s32[]{:S(2)}) async-start(), calls=%async_computation | async-start | bytes 262144 | tf_op jit(solution)/shard_map/psum | solution.py:70
  7.3 32.7 %copy-start.5 = (bf16[128,256]{1,0:T(8,128)(2,1)S(1)}, bf16[128,256]{1,0:T(8,128)(2,1)}, u32[]{:S(2)}) copy-start(bf16[128,256]{1,0:T(8,128)(2,1)} %param.6) | copy-start | bytes 196612
  66.3 0.6 copy-start.1
  66.9 26.8 %copy-start.6 = (bf16[128,512]{1,0:T(8,128)(2,1)S(1)}, bf16[128,512]{1,0:T(8,128)(2,1)}, u32[]{:S(2)}) copy-start(bf16[128,512]{1,0:T(8,128)(2,1)} %param.9) | copy-start | bytes 393220
  93.2 0.6 copy-start.2
  151.5 0.6 copy-start.3
  178.4 0.6 copy-start.4
  178.4 0.7 slice-start.1
  179.1 0.7 slice-start.3
  179.8 0.7 slice-start.5
  180.5 0.7 slice-start.7
  181.2 0.7 slice-start.2
  181.2 0.7 slice-start.4
  181.2 0.7 slice-start.6
  181.2 0.7 slice-start
Sparse Core Ops, SparseCore 0:
  191.0 15.4 all-reduce.1
where the time goes:
time: 216 us; the launch traced here: 215 us
  blocking collectives  175 us (81%)
  waiting for transfers between devices  15.7 us (7%)
  between operations  13.5 us (6%)
  local copies, waits for them, and re-layouts  8 us (4%)
    all_gather x8, blocking collectives, merged_2(): pieces = jax.tree.map(lambda part: lax.all_gather(part, axis), value)  111 us
    all_gather x1, blocking collectives, per_device(): lax.all_gather(text_student_own, 'group', axis=0, tiled=True)  32.6 us
    all_gather x1, blocking collectives, per_device(): lax.all_gather(text_teacher_own, 'group', axis=0, tiled=True)  31.3 us
    psum x1, waiting for transfers between devices, per_device(): return lax.psum(partial_image, 'blk')  15.7 us
  transfers between devices with their start and end apart: 1, of which 1 were waited for; matrix products, arithmetic and copies ran while one was open for 0% of the time, Pallas kernels for 0%

commit v1 on v0

--- a/solution.py
+++ b/solution.py
@@ -1,6 +1,10 @@
+import functools
+
 import jax
 import jax.numpy as jnp
 from jax import lax
+from jax.experimental import pallas as pl
+from jax.experimental.pallas import tpu as pltpu
 from jax.sharding import PartitionSpec as P
 
 
@@ -24,7 +28,7 @@
     return tuple(merged)
 
 
-def per_device(img_student, txt_student, img_teacher, txt_teacher):
+def general(img_student, txt_student, img_teacher, txt_teacher):
     half_rows = img_student.shape[0] // 2
     side = lax.axis_index("blk")
     begin = side * half_rows
@@ -70,17 +74,336 @@
     return lax.psum(partial_image, "blk")
 
 
+MESH = pl.DeviceIdType.MESH
+SQUARE = 4
+
+
+def exchange_kernel(
+    img_s_hbm, txt_s_hbm, img_t_hbm, txt_t_hbm, out_ref,
+    txt_s, txt_t, img_s, img_t,
+    er_s, er_t, ec_s, ec_t,
+    col_stats, row_send, row_recv, part_a, part_b, part_c,
+    local_sem,
+    txt_send, txt_recv, fwd_send, fwd_recv,
+    img_send, img_recv,
+    col_send, col_recv, row_send_sem, row_recv_sem,
+    a_send, a_recv, b_send, b_recv,
+):
+    rows = img_s.shape[0]
+    half = rows // 2
+    group = lax.axis_index("group")
+    core = lax.axis_index("blk")
+    x = lax.rem(group, 2)
+    b = lax.rem(group // 2, 2)
+    a = group // 4
+
+    def chip(d, other_half=0):
+        return (
+            lax.rem(a + other_half, 2) * 4
+            + lax.rem(b + d // 2, 2) * 2
+            + lax.rem(x + d % 2, 2)
+        )
+
+    def device(chip_index, core_index):
+        return {"blk": core_index, "group": chip_index}
+
+    sibling = device(group, 1 - core)
+    partner = chip(0, 1)
+
+    def remote(src, dst, send, recv, target):
+        return pltpu.make_async_remote_copy(
+            src_ref=src, dst_ref=dst, send_sem=send, recv_sem=recv,
+            device_id=target, device_id_type=MESH,
+        )
+
+    mine = pl.ds(pl.multiple_of(core * half, half), half)
+    theirs = pl.ds(pl.multiple_of((1 - core) * half, half), half)
+
+    own = [
+        pltpu.make_async_copy(txt_s_hbm, txt_s.at[0], local_sem.at[0]),
+        pltpu.make_async_copy(txt_t_hbm, txt_t.at[0], local_sem.at[1]),
+    ]
+    own_img = [
+        pltpu.make_async_copy(img_s_hbm, img_s, local_sem.at[2]),
+        pltpu.make_async_copy(img_t_hbm, img_t, local_sem.at[3]),
+    ]
+    for copy in own:
+        copy.start()
+
+    @pl.when(core == 0)
+    def _():
+        for copy in own_img:
+            copy.start()
+
+    barrier = pltpu.get_barrier_semaphore()
+    greeted = [sibling, device(partner, core), device(partner, 1 - core)]
+    for d in range(1, SQUARE):
+        greeted += [device(chip(d), core), device(chip(d), 1 - core)]
+    for target in greeted:
+        pl.semaphore_signal(barrier, inc=1, device_id=target, device_id_type=MESH)
+    pl.semaphore_wait(barrier, len(greeted))
+
+    img_out = [
+        remote(img_s_hbm.at[mine], img_s.at[mine], img_send.at[0], img_recv.at[0, core], device(partner, 1)),
+        remote(img_t_hbm.at[mine], img_t.at[mine], img_send.at[1], img_recv.at[1, core], device(partner, 1)),
+    ]
+    text_out = {}
+    for d in range(1, SQUARE):
+        text_out[d] = [
+            remote(txt_s_hbm.at[mine], txt_s.at[d, mine], txt_send.at[0, d], txt_recv.at[0, d], device(chip(d), core)),
+            remote(txt_t_hbm.at[mine], txt_t.at[d, mine], txt_send.at[1, d], txt_recv.at[1, d], device(chip(d), core)),
+        ]
+    img_out[0].start()
+    for copy in text_out[1] + text_out[2]:
+        copy.start()
+    img_out[1].start()
+    for copy in text_out[3]:
+        copy.start()
+
+    forward = {}
+
+    def pass_on(d):
+        forward[d] = []
+        for which, ref in ((0, txt_s), (1, txt_t)):
+            text_out[d][which].wait_recv()
+            copy = remote(
+                ref.at[d, mine], ref.at[d, mine],
+                fwd_send.at[which, d], fwd_recv.at[which, d], sibling,
+            )
+            copy.start()
+            forward[d].append(copy)
+
+    contract = (((1,), (1,)), ((), ()))
+    row_stats = []
+
+    def tile(d):
+        if d == 0:
+            for copy in own:
+                copy.wait()
+        else:
+            for which, ref in ((0, txt_s), (1, txt_t)):
+                remote(
+                    ref.at[d, theirs], ref.at[d, theirs],
+                    fwd_send.at[which, d], fwd_recv.at[which, d], sibling,
+                ).wait_recv()
+        found = []
+        for which, (img, txt, er, ec) in enumerate(
+            ((img_s, txt_s, er_s, ec_s), (img_t, txt_t, er_t, ec_t))
+        ):
+            logits = lax.dot_general(
+                img[...], txt[d], contract, preferred_element_type=jnp.float32
+            )
+            row_high = jnp.max(logits, axis=1, keepdims=True)
+            row_exp = jnp.exp(logits - row_high)
+            er[d] = row_exp
+            found.append((row_high, jnp.sum(row_exp, axis=1, keepdims=True)))
+            column_high = jnp.max(logits, axis=0, keepdims=True)
+            column_exp = jnp.exp(logits - column_high)
+            ec[d] = column_exp
+            at = which * SQUARE + d
+            col_stats[0, at : at + 1, :] = column_high
+            col_stats[0, 8 + at : 9 + at, :] = jnp.sum(column_exp, axis=0, keepdims=True)
+        row_stats.append(found)
+
+    pass_on(1)
+
+    @pl.when(core == 0)
+    def _():
+        for copy in own_img:
+            copy.wait()
+
+    @pl.when(core == 1)
+    def _():
+        for h in range(2):
+            at = pl.ds(h * half, half)
+            for which, ref in ((0, img_s), (1, img_t)):
+                remote(
+                    ref.at[at], ref.at[at], img_send.at[which], img_recv.at[which, h], device(partner, 1)
+                ).wait_recv()
+
+    tile(0)
+    pass_on(2)
+    tile(1)
+    pass_on(3)
+    tile(2)
+    tile(3)
+
+    col_out = []
+    for d in range(SQUARE):
+        for e in range(2):
+            slot = 2 * d + e
+            if slot:
+                target = device(chip(d), core if e == 0 else 1 - core)
+                copy = remote(
+                    col_stats.at[0], col_stats.at[slot], col_send.at[slot], col_recv.at[slot], target
+                )
+                copy.start()
+                col_out.append(copy)
+
+    lane = lax.broadcasted_iota(jnp.int32, (rows, rows), 1)
+    packed = jnp.zeros((rows, rows), jnp.float32)
+    scale = []
+    local = []
+    for which in range(2):
+        highs = [found[which][0] for found in row_stats]
+        high = functools.reduce(jnp.maximum, highs)
+        scales = [jnp.exp(h - high) for h in highs]
+        total = sum(s * found[which][1] for s, found in zip(scales, row_stats))
+        packed = jnp.where(lane == 2 * which, high, packed)
+        packed = jnp.where(lane == 2 * which + 1, total, packed)
+        scale.append(scales)
+        local.append((high, total))
+    row_send[...] = jnp.transpose(packed)[:8, :]
+    row_out = remote(
+        row_send, row_recv, row_send_sem.at[0], row_recv_sem.at[0], device(partner, 1 - core)
+    )
+    row_out.start()
+
+    for copy in col_out:
+        copy.wait_recv()
+    highs, sums = [], []
+    for d in range(SQUARE):
+        for e in range(2):
+            slot = 2 * d + e
+            value = col_stats[slot]
+            order = [SQUARE * w + (k ^ d) for w in range(2) for k in range(SQUARE)]
+            if d:
+                highs.append(jnp.concatenate([value[k : k + 1] for k in order], axis=0))
+                sums.append(jnp.concatenate([value[8 + k : 9 + k] for k in order], axis=0))
+            else:
+                highs.append(value[:8])
+                sums.append(value[8:])
+    column_high = functools.reduce(jnp.maximum, highs)
+    column_total = sum(s * jnp.exp(h - column_high) for h, s in zip(highs, sums))
+    column_factor = 0.5 * jnp.exp(highs[0] - column_high) / column_total
+
+    row_out.wait_recv()
+    other = jnp.transpose(jnp.concatenate([row_recv[...]] * (rows // 8), axis=0))
+    row_factor = []
+    for which in range(2):
+        high, total = local[which]
+        other_high = other[:, 2 * which : 2 * which + 1]
+        other_total = other[:, 2 * which + 1 : 2 * which + 2]
+        top = jnp.maximum(high, other_high)
+        everything = total * jnp.exp(high - top) + other_total * jnp.exp(other_high - top)
+        common = 0.5 * jnp.exp(high - top) / everything
+        row_factor.append([common * s for s in scale[which]])
+
+    share = None
+    for d in range(SQUARE):
+        weights = (
+            er_s[d] * row_factor[0][d] - er_t[d] * row_factor[1][d]
+        ) + (
+            ec_s[d] * column_factor[d : d + 1] - ec_t[d] * column_factor[SQUARE + d : SQUARE + d + 1]
+        )
+        product = jnp.dot(
+            weights.astype(jnp.bfloat16), txt_s[d], preferred_element_type=jnp.float32
+        )
+        share = product if share is None else share + product
+
+    a_out = remote(part_a, part_a, a_send.at[0], a_recv.at[0], sibling)
+    b_out = []
+    for h in range(2):
+        at = pl.ds(h * half, half)
+        b_out.append(
+            remote(part_c.at[at], part_b.at[at], b_send.at[h], b_recv.at[0], device(partner, h))
+        )
+
+    @pl.when(core == 0)
+    def _():
+        part_a[...] = share
+        a_out.start()
+
+    @pl.when(core == 1)
+    def _():
+        part_c[...] = share
+        for copy in b_out:
+            copy.start()
+
+    remote(part_b.at[mine], part_b.at[mine], b_send.at[0], b_recv.at[0], sibling).wait_recv()
+    b_forward = remote(part_b.at[mine], part_b.at[mine], b_send.at[2], b_recv.at[1], sibling)
+    b_forward.start()
+
+    @pl.when(core == 1)
+    def _():
+        a_out.wait_recv()
+
+    remote(part_b.at[theirs], part_b.at[theirs], b_send.at[2], b_recv.at[1], sibling).wait_recv()
+    out_ref[...] = part_a[...] + part_b[...]
+
+    for copy in img_out + text_out[1] + text_out[2] + text_out[3] + col_out:
+        copy.wait_send()
+    for d in range(1, SQUARE):
+        for copy in forward[d]:
+            copy.wait_send()
+    row_out.wait_send()
+    b_forward.wait_send()
+
+    @pl.when(core == 0)
+    def _():
+        a_out.wait_send()
+
+    @pl.when(core == 1)
+    def _():
+        for copy in b_out:
+            copy.wait_send()
+
+
+def eight_chips(img_student, txt_student, img_teacher, txt_teacher):
+    rows, narrow = img_student.shape
+    wide = img_teacher.shape[1]
+    dma = pltpu.SemaphoreType.DMA
+    tiles = pltpu.VMEM((SQUARE, rows, rows), jnp.float32)
+    partial = pltpu.VMEM((rows, narrow), jnp.float32)
+    return pl.pallas_call(
+        exchange_kernel,
+        out_shape=jax.ShapeDtypeStruct((rows, narrow), jnp.float32),
+        in_specs=[pl.BlockSpec(memory_space=pl.ANY)] * 4,
+        out_specs=pl.BlockSpec(memory_space=pltpu.VMEM),
+        scratch_shapes=[
+            pltpu.VMEM((SQUARE, rows, narrow), jnp.bfloat16),
+            pltpu.VMEM((SQUARE, rows, wide), jnp.bfloat16),
+            pltpu.VMEM((rows, narrow), jnp.bfloat16),
+            pltpu.VMEM((rows, wide), jnp.bfloat16),
+            tiles, tiles, tiles, tiles,
+            pltpu.VMEM((2 * SQUARE, 16, rows), jnp.float32),
+            pltpu.VMEM((8, rows), jnp.float32),
+            pltpu.VMEM((8, rows), jnp.float32),
+            partial, partial, partial,
+            dma((4,)),
+            dma((2, SQUARE)), dma((2, SQUARE)), dma((2, SQUARE)), dma((2, SQUARE)),
+            dma((2,)), dma((2, 2)),
+            dma((2 * SQUARE,)), dma((2 * SQUARE,)), dma((1,)), dma((1,)),
+            dma((1,)), dma((1,)), dma((3,)), dma((2,)),
+        ],
+        compiler_params=pltpu.CompilerParams(
+            collective_id=0, has_side_effects=True, vmem_limit_bytes=32 * 1024 * 1024
+        ),
+        cost_estimate=pl.CostEstimate(
+            flops=2 * rows * SQUARE * rows * (2 * narrow + wide),
+            bytes_accessed=8 * rows * (narrow + wide),
+            transcendentals=4 * SQUARE * rows * rows,
+        ),
+    )(img_student, txt_student, img_teacher, txt_teacher)
+
+
 def solution(mesh):
-    placed = (
-        P(("parts", "group"), None),
-        P(("parts", "group"), None),
-        P(("parts", "group"), None),
-        P(("parts", "group"), None),
-    )
+    placed = P(("parts", "group"), None)
+
+    def per_device(img_student, txt_student, img_teacher, txt_teacher):
+        fits = (
+            mesh.shape["group"] == 8
+            and mesh.shape["blk"] == 2
+            and img_student.shape[0] == 128
+            and txt_student.shape[0] == 128
+        )
+        run = eight_chips if fits else general
+        return run(img_student, txt_student, img_teacher, txt_teacher)
+
     return jax.shard_map(
         per_device,
         mesh=mesh,
-        in_specs=placed,
-        out_specs=P(("parts", "group"), None),
+        in_specs=(placed,) * 4,
+        out_specs=placed,
         check_vma=False,
     )

time: 216 us -> 30.5 us (0.14)
  blocking collectives: 175 us -> 0 us
  Pallas kernels: 0 us -> 26.1 us
  waiting for transfers between devices: 15.7 us -> 0 us
  between operations: 13.5 us -> 0.01 us
  local copies, waits for them, and re-layouts: 8 us -> 4.14 us
    all_gather x10 -> x0, blocking collectives: 175 us -> none  [the longest x8 111 us: merged_2(): pieces = jax.tree.map(lambda part: lax.all_gather(part, axis), value)]
    pallas_call x0 -> x1, Pallas kernels: none -> 26.1 us  [eight_chips(): pl.pallas_call(exchange_kernel, out_shape=jax.ShapeDtypeStruct((rows, nar...]
    psum x1 -> x0, waiting for transfers between devices: 15.7 us -> none  [per_device(): return lax.psum(partial_image, 'blk')]
    slice x16 -> x0, local copies, waits for them, and re-layouts: 2.94 us -> none  [the longest x8 2.25 us: merged_2(): tail = jax.tree.map(lambda part: part[1:], pieces)]
  transfers between devices with their start and end apart: 1 -> 0, of which waited for: 1 -> 0; matrix products, arithmetic and copies ran while one was open for 0% -> 0% of each run, Pallas kernels for 0% -> 0%
where the time goes in v1:
time: 30.5 us; the launch traced here: 30.3 us
  Pallas kernels  26.1 us (86%)
  local copies, waits for them, and re-layouts  4.14 us (14%)
    pallas_call x1, Pallas kernels, eight_chips(): pl.pallas_call(exchange_kernel, out_shape=jax.ShapeDtypeStruct((rows, nar...  26.1 us
    unnamed x9, local copies, waits for them, and re-layouts  4.14 us

profile of v1, /device:TPU:0, one launch (start us, length us, event | category | flops | bytes accessed | tf_op | source)
XLA Modules:
  0.0 30.3 jit_solution(5410621174765640670)
XLA Ops:
  0.0 0.0 copy-start
  0.0 0.9 %copy-done = bf16[128,512]{1,0:T(8,128)(2,1)S(1)} copy-done((bf16[128,512]{1,0:T(8,128)(2,1)S(1)}, bf16[128,512]{1,0:T(8,128)(2,1)}, u32[]{:S(2)}) %copy-start) | copy-done | bytes 131096
  0.9 0.0 copy-start.1
  0.9 0.9 %copy-done.1 = bf16[128,512]{1,0:T(8,128)(2,1)S(1)} copy-done((bf16[128,512]{1,0:T(8,128)(2,1)S(1)}, bf16[128,512]{1,0:T(8,128)(2,1)}, u32[]{:S(2)}) %copy-start.1) | copy-done | bytes 131096
  1.8 0.0 copy-start.2
  1.8 0.8 %copy-done.2 = bf16[128,256]{1,0:T(8,128)(2,1)S(1)} copy-done((bf16[128,256]{1,0:T(8,128)(2,1)S(1)}, bf16[128,256]{1,0:T(8,128)(2,1)}, u32[]{:S(2)}) %copy-start.2) | copy-done | bytes 65560
  2.6 0.0 copy-start.3
  2.7 0.8 %copy-done.3 = bf16[128,256]{1,0:T(8,128)(2,1)S(1)} copy-done((bf16[128,256]{1,0:T(8,128)(2,1)S(1)}, bf16[128,256]{1,0:T(8,128)(2,1)}, u32[]{:S(2)}) %copy-start.3) | copy-done | bytes 65560
  3.5 26.1 %shard_map.46 = f32[128,256]{1,0:T(8,128)S(1)} custom-call(bf16[128,256]{1,0:T(8,128)(2,1)S(1)} %copy-done.2, bf16[128,256]{1,0:T(8,128)(2,1)S(1)} %copy-done.3, bf16[128,512]{1,0:T(8,128)(2,1)S(1)} %copy-done, bf16[128,512]{1,0:T(8,128)(2,1)S(1)} %copy-done.1), custom_call_target="tpu_custom_call" | custom-call | flops 134217728 | bytes 786432 | tf_op jit(solution)/shard_map/pallas_call | solution.py:358
  29.6 0.7 %copy.6 = f32[128,256]{1,0:T(8,128)} copy(f32[128,256]{1,0:T(8,128)S(1)} %shard_map.46) | data formatting | bytes 262144
Async XLA Ops:
  0.0 0.9 %copy-start = (bf16[128,512]{1,0:T(8,128)(2,1)S(1)}, bf16[128,512]{1,0:T(8,128)(2,1)}, u32[]{:S(2)}) copy-start(bf16[128,512]{1,0:T(8,128)(2,1)} %img_t_hbm.1) | copy-start | bytes 393220
  0.9 0.9 %copy-start.1 = (bf16[128,512]{1,0:T(8,128)(2,1)S(1)}, bf16[128,512]{1,0:T(8,128)(2,1)}, u32[]{:S(2)}) copy-start(bf16[128,512]{1,0:T(8,128)(2,1)} %txt_t_hbm.1) | copy-start | bytes 393220
  1.8 0.8 %copy-start.2 = (bf16[128,256]{1,0:T(8,128)(2,1)S(1)}, bf16[128,256]{1,0:T(8,128)(2,1)}, u32[]{:S(2)}) copy-start(bf16[128,256]{1,0:T(8,128)(2,1)} %img_s_hbm.1) | copy-start | bytes 196612
  2.6 0.8 %copy-start.3 = (bf16[128,256]{1,0:T(8,128)(2,1)S(1)}, bf16[128,256]{1,0:T(8,128)(2,1)}, u32[]{:S(2)}) copy-start(bf16[128,256]{1,0:T(8,128)(2,1)} %txt_s_hbm.1) | copy-start | bytes 196612

commit v2 on v1

--- a/solution.py
+++ b/solution.py
@@ -358,7 +358,7 @@
     return pl.pallas_call(
         exchange_kernel,
         out_shape=jax.ShapeDtypeStruct((rows, narrow), jnp.float32),
-        in_specs=[pl.BlockSpec(memory_space=pl.ANY)] * 4,
+        in_specs=[pl.BlockSpec(memory_space=pltpu.HBM)] * 4,
         out_specs=pl.BlockSpec(memory_space=pltpu.VMEM),
         scratch_shapes=[
             pltpu.VMEM((SQUARE, rows, narrow), jnp.bfloat16),
@@ -377,7 +377,7 @@
             dma((1,)), dma((1,)), dma((3,)), dma((2,)),
         ],
         compiler_params=pltpu.CompilerParams(
-            collective_id=0, has_side_effects=True, vmem_limit_bytes=32 * 1024 * 1024
+            collective_id=0, has_side_effects=True, vmem_limit_bytes=60 * 1024 * 1024
         ),
         cost_estimate=pl.CostEstimate(
             flops=2 * rows * SQUARE * rows * (2 * narrow + wide),

time: 30.5 us -> 28.2 us (0.925)
  local copies, waits for them, and re-layouts: 4.14 us -> 1.57 us
  Pallas kernels: 26.1 us -> 26.5 us
    unnamed x9 -> x1, local copies, waits for them, and re-layouts: 4.14 us -> 1.57 us
    pallas_call x1, Pallas kernels: 26.1 us -> 26.5 us  [eight_chips(): pl.pallas_call(exchange_kernel, out_shape=jax.ShapeDtypeStruct((rows, nar...]
where the time goes in v2:
time: 28.2 us; the launch traced here: 28.1 us
  Pallas kernels  26.5 us (94%)
  local copies, waits for them, and re-layouts  1.57 us (6%)
    pallas_call x1, Pallas kernels, eight_chips(): pl.pallas_call(exchange_kernel, out_shape=jax.ShapeDtypeStruct((rows, nar...  26.5 us
    unnamed x1, local copies, waits for them, and re-layouts  1.57 us

profile of v2, /device:TPU:0, one launch (start us, length us, event | category | flops | bytes accessed | tf_op | source)
XLA Modules:
  0.0 28.1 jit_solution(6194397727658833379)
XLA Ops:
  0.0 26.5 %shard_map.46 = f32[128,256]{1,0:T(8,128)} custom-call(bf16[128,256]{1,0:T(8,128)(2,1)} %img_s_hbm.1, bf16[128,256]{1,0:T(8,128)(2,1)} %txt_s_hbm.1, bf16[128,512]{1,0:T(8,128)(2,1)} %img_t_hbm.1, bf16[128,512]{1,0:T(8,128)(2,1)} %txt_t_hbm.1), custom_call_target="tpu_custom_call" | custom-call | flops 134217728 | bytes 786432 | tf_op jit(solution)/shard_map/pallas_call | solution.py:358
  26.5 1.6 %copy.6 = f32[128,256]{1,0:T(8,128)} copy(f32[128,256]{1,0:T(8,128)} %shard_map.46) | data formatting | bytes 262144

commit v3 on v2

--- a/solution.py
+++ b/solution.py
@@ -153,11 +153,7 @@
             remote(txt_s_hbm.at[mine], txt_s.at[d, mine], txt_send.at[0, d], txt_recv.at[0, d], device(chip(d), core)),
             remote(txt_t_hbm.at[mine], txt_t.at[d, mine], txt_send.at[1, d], txt_recv.at[1, d], device(chip(d), core)),
         ]
-    img_out[0].start()
-    for copy in text_out[1] + text_out[2]:
-        copy.start()
-    img_out[1].start()
-    for copy in text_out[3]:
+    for copy in text_out[3] + img_out + text_out[1] + text_out[2]:
         copy.start()
 
     forward = {}
@@ -316,7 +312,7 @@
 
     @pl.when(core == 1)
     def _():
-        part_c[...] = share
+        part_c[...] = share.astype(part_c.dtype)
         for copy in b_out:
             copy.start()
 
@@ -329,7 +325,7 @@
         a_out.wait_recv()
 
     remote(part_b.at[theirs], part_b.at[theirs], b_send.at[2], b_recv.at[1], sibling).wait_recv()
-    out_ref[...] = part_a[...] + part_b[...]
+    out_ref[...] = part_a[...] + part_b[...].astype(jnp.float32)
 
     for copy in img_out + text_out[1] + text_out[2] + text_out[3] + col_out:
         copy.wait_send()
@@ -355,9 +351,10 @@
     dma = pltpu.SemaphoreType.DMA
     tiles = pltpu.VMEM((SQUARE, rows, rows), jnp.float32)
     partial = pltpu.VMEM((rows, narrow), jnp.float32)
+    travelling = pltpu.VMEM((rows, narrow), jnp.bfloat16)
     return pl.pallas_call(
         exchange_kernel,
-        out_shape=jax.ShapeDtypeStruct((rows, narrow), jnp.float32),
+        out_shape=pltpu.VMEM((rows, narrow), jnp.float32),
         in_specs=[pl.BlockSpec(memory_space=pltpu.HBM)] * 4,
         out_specs=pl.BlockSpec(memory_space=pltpu.VMEM),
         scratch_shapes=[
@@ -369,7 +366,7 @@
             pltpu.VMEM((2 * SQUARE, 16, rows), jnp.float32),
             pltpu.VMEM((8, rows), jnp.float32),
             pltpu.VMEM((8, rows), jnp.float32),
-            partial, partial, partial,
+            partial, travelling, travelling,
             dma((4,)),
             dma((2, SQUARE)), dma((2, SQUARE)), dma((2, SQUARE)), dma((2, SQUARE)),
             dma((2,)), dma((2, 2)),

time: 28.2 us -> 24.6 us (0.87)
  Pallas kernels: 26.5 us -> 23.8 us
  local copies, waits for them, and re-layouts: 1.57 us -> 0.66 us
    pallas_call x1, Pallas kernels: 26.5 us -> 23.8 us  [eight_chips(): pl.pallas_call(exchange_kernel, out_shape=pltpu.VMEM((rows, narrow), jnp....]
    unnamed x1, local copies, waits for them, and re-layouts: 1.57 us -> 0.66 us
where the time goes in v3:
time: 24.6 us; the launch traced here: 24.4 us
  Pallas kernels  23.8 us (97%)
  local copies, waits for them, and re-layouts  0.66 us (3%)
    pallas_call x1, Pallas kernels, eight_chips(): pl.pallas_call(exchange_kernel, out_shape=pltpu.VMEM((rows, narrow), jnp....  23.8 us
    unnamed x1, local copies, waits for them, and re-layouts  0.66 us

profile of v3, /device:TPU:0, one launch (start us, length us, event | category | flops | bytes accessed | tf_op | source)
XLA Modules:
  0.0 24.4 jit_solution(5984965878333024087)
XLA Ops:
  0.0 23.8 %shard_map.46 = f32[128,256]{1,0:T(8,128)S(1)} custom-call(bf16[128,256]{1,0:T(8,128)(2,1)} %img_s_hbm.1, bf16[128,256]{1,0:T(8,128)(2,1)} %txt_s_hbm.1, bf16[128,512]{1,0:T(8,128)(2,1)} %img_t_hbm.1, bf16[128,512]{1,0:T(8,128)(2,1)} %txt_t_hbm.1), custom_call_target="tpu_custom_call" | custom-call | flops 134217728 | bytes 786432 | tf_op jit(solution)/shard_map/pallas_call | solution.py:355
  23.8 0.7 %copy.6 = f32[128,256]{1,0:T(8,128)} copy(f32[128,256]{1,0:T(8,128)S(1)} %shard_map.46) | data formatting | bytes 262144

commit v4 on v3

--- a/solution.py
+++ b/solution.py
@@ -151,23 +151,32 @@
     for d in range(1, SQUARE):
         text_out[d] = [
             remote(txt_s_hbm.at[mine], txt_s.at[d, mine], txt_send.at[0, d], txt_recv.at[0, d], device(chip(d), core)),
-            remote(txt_t_hbm.at[mine], txt_t.at[d, mine], txt_send.at[1, d], txt_recv.at[1, d], device(chip(d), core)),
         ]
-    for copy in text_out[3] + img_out + text_out[1] + text_out[2]:
+    for d in (1, 2):
+        text_out[d].append(
+            remote(txt_t_hbm.at[mine], txt_t.at[d, mine], txt_send.at[1, d], txt_recv.at[1, d], device(chip(d), core))
+        )
+    text_out[3].append(remote(
+        txt_t.at[2, mine], txt_t.at[3, mine], txt_send.at[1, 3], txt_recv.at[1, 3], device(chip(1), core)
+    ))
+    for copy in (
+        [text_out[2][1], text_out[3][0]] + img_out + [text_out[1][1], text_out[1][0], text_out[2][0]]
+    ):
         copy.start()
 
     forward = {}
 
-    def pass_on(d):
-        forward[d] = []
-        for which, ref in ((0, txt_s), (1, txt_t)):
-            text_out[d][which].wait_recv()
-            copy = remote(
-                ref.at[d, mine], ref.at[d, mine],
-                fwd_send.at[which, d], fwd_recv.at[which, d], sibling,
-            )
-            copy.start()
-            forward[d].append(copy)
+    def pass_on(d, which):
+        ref = (txt_s, txt_t)[which]
+        text_out[d][which].wait_recv()
+        if (d, which) == (2, 1):
+            text_out[3][1].start()
+        copy = remote(
+            ref.at[d, mine], ref.at[d, mine],
+            fwd_send.at[which, d], fwd_recv.at[which, d], sibling,
+        )
+        copy.start()
+        forward[d, which] = copy
 
     contract = (((1,), (1,)), ((), ()))
     row_stats = []
@@ -201,7 +210,10 @@
             col_stats[0, 8 + at : 9 + at, :] = jnp.sum(column_exp, axis=0, keepdims=True)
         row_stats.append(found)
 
-    pass_on(1)
+    pass_on(2, 1)
+    pass_on(1, 1)
+    pass_on(1, 0)
+    pass_on(2, 0)
 
     @pl.when(core == 0)
     def _():
@@ -218,9 +230,9 @@
                 ).wait_recv()
 
     tile(0)
-    pass_on(2)
+    pass_on(3, 0)
+    pass_on(3, 1)
     tile(1)
-    pass_on(3)
     tile(2)
     tile(3)
 
@@ -329,9 +341,8 @@
 
     for copy in img_out + text_out[1] + text_out[2] + text_out[3] + col_out:
         copy.wait_send()
-    for d in range(1, SQUARE):
-        for copy in forward[d]:
-            copy.wait_send()
+    for copy in forward.values():
+        copy.wait_send()
     row_out.wait_send()
     b_forward.wait_send()
 

time: 24.6 us -> 24.8 us (level)
    pallas_call x1, Pallas kernels: 23.8 us -> 24 us  [eight_chips(): pl.pallas_call(exchange_kernel, out_shape=pltpu.VMEM((rows, narrow), jnp....]
where the time goes in v4:
time: 24.8 us; the launch traced here: 24.7 us
  Pallas kernels  24 us (97%)
  local copies, waits for them, and re-layouts  0.66 us (3%)
    pallas_call x1, Pallas kernels, eight_chips(): pl.pallas_call(exchange_kernel, out_shape=pltpu.VMEM((rows, narrow), jnp....  24 us
    unnamed x1, local copies, waits for them, and re-layouts  0.66 us

profile of v4, /device:TPU:0, one launch (start us, length us, event | category | flops | bytes accessed | tf_op | source)
XLA Modules:
  0.0 24.7 jit_solution(17916259408814986547)
XLA Ops:
  0.0 24.0 %shard_map.46 = f32[128,256]{1,0:T(8,128)S(1)} custom-call(bf16[128,256]{1,0:T(8,128)(2,1)} %img_s_hbm.1, bf16[128,256]{1,0:T(8,128)(2,1)} %txt_s_hbm.1, bf16[128,512]{1,0:T(8,128)(2,1)} %img_t_hbm.1, bf16[128,512]{1,0:T(8,128)(2,1)} %txt_t_hbm.1), custom_call_target="tpu_custom_call" | custom-call | flops 134217728 | bytes 786432 | tf_op jit(solution)/shard_map/pallas_call | solution.py:366
  24.0 0.7 %copy.6 = f32[128,256]{1,0:T(8,128)} copy(f32[128,256]{1,0:T(8,128)S(1)} %shard_map.46) | data formatting | bytes 262144

commit v5 on v4

--- a/solution.py
+++ b/solution.py
@@ -159,10 +159,12 @@
     text_out[3].append(remote(
         txt_t.at[2, mine], txt_t.at[3, mine], txt_send.at[1, 3], txt_recv.at[1, 3], device(chip(1), core)
     ))
-    for copy in (
-        [text_out[2][1], text_out[3][0]] + img_out + [text_out[1][1], text_out[1][0], text_out[2][0]]
-    ):
+    ahead = [text_out[1][1], text_out[1][0], text_out[2][1], text_out[3][0]]
+    for copy in img_out + ahead:
         copy.start()
+    for copy in img_out:
+        copy.wait_send()
+    text_out[2][0].start()
 
     forward = {}
 
@@ -339,7 +341,7 @@
     remote(part_b.at[theirs], part_b.at[theirs], b_send.at[2], b_recv.at[1], sibling).wait_recv()
     out_ref[...] = part_a[...] + part_b[...].astype(jnp.float32)
 
-    for copy in img_out + text_out[1] + text_out[2] + text_out[3] + col_out:
+    for copy in text_out[1] + text_out[2] + text_out[3] + col_out:
         copy.wait_send()
     for copy in forward.values():
         copy.wait_send()

time: 24.8 us -> 23.8 us (0.960)
  Pallas kernels: 24 us -> 23 us
    pallas_call x1, Pallas kernels: 24 us -> 23 us  [eight_chips(): pl.pallas_call(exchange_kernel, out_shape=pltpu.VMEM((rows, narrow), jnp....]
where the time goes in v5:
time: 23.8 us; the launch traced here: 23.7 us
  Pallas kernels  23 us (97%)
  local copies, waits for them, and re-layouts  0.66 us (3%)
    pallas_call x1, Pallas kernels, eight_chips(): pl.pallas_call(exchange_kernel, out_shape=pltpu.VMEM((rows, narrow), jnp....  23 us
    unnamed x1, local copies, waits for them, and re-layouts  0.66 us

profile of v5, /device:TPU:0, one launch (start us, length us, event | category | flops | bytes accessed | tf_op | source)
XLA Modules:
  0.0 23.7 jit_solution(8187976252770847073)
XLA Ops:
  0.0 23.0 %shard_map.46 = f32[128,256]{1,0:T(8,128)S(1)} custom-call(bf16[128,256]{1,0:T(8,128)(2,1)} %img_s_hbm.1, bf16[128,256]{1,0:T(8,128)(2,1)} %txt_s_hbm.1, bf16[128,512]{1,0:T(8,128)(2,1)} %img_t_hbm.1, bf16[128,512]{1,0:T(8,128)(2,1)} %txt_t_hbm.1), custom_call_target="tpu_custom_call" | custom-call | flops 134217728 | bytes 786432 | tf_op jit(solution)/shard_map/pallas_call | solution.py:368
  23.0 0.7 %copy.6 = f32[128,256]{1,0:T(8,128)} copy(f32[128,256]{1,0:T(8,128)S(1)} %shard_map.46) | data formatting | bytes 262144

commit v6 on v5

--- a/solution.py
+++ b/solution.py
@@ -182,6 +182,7 @@
 
     contract = (((1,), (1,)), ((), ()))
     row_stats = []
+    own_highs = [[], []]
 
     def tile(d):
         if d == 0:
@@ -208,8 +209,10 @@
             column_exp = jnp.exp(logits - column_high)
             ec[d] = column_exp
             at = which * SQUARE + d
-            col_stats[0, at : at + 1, :] = column_high
-            col_stats[0, 8 + at : 9 + at, :] = jnp.sum(column_exp, axis=0, keepdims=True)
+            own_highs[which].append(column_high)
+            col_stats[0, at : at + 1, :] = column_high + jnp.log(
+                jnp.sum(column_exp, axis=0, keepdims=True)
+            )
         row_stats.append(found)
 
     pass_on(2, 1)
@@ -271,21 +274,19 @@
 
     for copy in col_out:
         copy.wait_recv()
-    highs, sums = [], []
+    totals = []
     for d in range(SQUARE):
         for e in range(2):
             slot = 2 * d + e
             value = col_stats[slot]
             order = [SQUARE * w + (k ^ d) for w in range(2) for k in range(SQUARE)]
             if d:
-                highs.append(jnp.concatenate([value[k : k + 1] for k in order], axis=0))
-                sums.append(jnp.concatenate([value[8 + k : 9 + k] for k in order], axis=0))
-            else:
-                highs.append(value[:8])
-                sums.append(value[8:])
-    column_high = functools.reduce(jnp.maximum, highs)
-    column_total = sum(s * jnp.exp(h - column_high) for h, s in zip(highs, sums))
-    column_factor = 0.5 * jnp.exp(highs[0] - column_high) / column_total
+                value = jnp.concatenate([value[k : k + 1] for k in order], axis=0)
+            totals.append(value)
+    column_high = functools.reduce(jnp.maximum, totals)
+    column_total = sum(jnp.exp(t - column_high) for t in totals)
+    own_high = jnp.concatenate(own_highs[0] + own_highs[1], axis=0)
+    column_factor = 0.5 * jnp.exp(own_high - column_high) / column_total
 
     row_out.wait_recv()
     other = jnp.transpose(jnp.concatenate([row_recv[...]] * (rows // 8), axis=0))
@@ -376,7 +377,7 @@
             pltpu.VMEM((rows, narrow), jnp.bfloat16),
             pltpu.VMEM((rows, wide), jnp.bfloat16),
             tiles, tiles, tiles, tiles,
-            pltpu.VMEM((2 * SQUARE, 16, rows), jnp.float32),
+            pltpu.VMEM((2 * SQUARE, 8, rows), jnp.float32),
             pltpu.VMEM((8, rows), jnp.float32),
             pltpu.VMEM((8, rows), jnp.float32),
             partial, travelling, travelling,

time: 23.8 us -> 23.6 us (level)
  no operation moved by 1% of the time
where the time goes in v6:
time: 23.6 us; the launch traced here: 23.5 us
  Pallas kernels  22.8 us (97%)
  local copies, waits for them, and re-layouts  0.66 us (3%)
    pallas_call x1, Pallas kernels, eight_chips(): pl.pallas_call(exchange_kernel, out_shape=pltpu.VMEM((rows, narrow), jnp....  22.8 us
    unnamed x1, local copies, waits for them, and re-layouts  0.66 us

profile of v6, /device:TPU:0, one launch (start us, length us, event | category | flops | bytes accessed | tf_op | source)
XLA Modules:
  0.0 23.5 jit_solution(2285994247363984957)
XLA Ops:
  0.0 22.8 %shard_map.46 = f32[128,256]{1,0:T(8,128)S(1)} custom-call(bf16[128,256]{1,0:T(8,128)(2,1)} %img_s_hbm.1, bf16[128,256]{1,0:T(8,128)(2,1)} %txt_s_hbm.1, bf16[128,512]{1,0:T(8,128)(2,1)} %img_t_hbm.1, bf16[128,512]{1,0:T(8,128)(2,1)} %txt_t_hbm.1), custom_call_target="tpu_custom_call" | custom-call | flops 134217728 | bytes 786432 | tf_op jit(solution)/shard_map/pallas_call | solution.py:369
  22.8 0.7 %copy.6 = f32[128,256]{1,0:T(8,128)} copy(f32[128,256]{1,0:T(8,128)S(1)} %shard_map.46) | data formatting | bytes 262144
